TPU v7x, 32 devices: a whole 2x2x4 slice. The times are simulated.
32 devices in a mesh: tm: 4 (over y, x), clus: 8 (over z, core).
Axes of the slice: x: 2, y: 2, z: 4, core: 2. Of those that a mesh axis runs over, the one named last changes fastest.
Arguments:
- embedding: bfloat16 [32768, 384], P(('tm', 'clus')), may hold values from -6 to 6
- cluster_of: int32 [32768], P(('tm', 'clus')), may hold values from 0 to 63, as said below
Outputs:
- mixed: bfloat16 [32768, 384], P(('tm', 'clus'))
Inputs may be any that keep to these rules, and one draw needn't show every extreme that they name: `cluster_of`: of the 1024 invoices of one device at most 64 belong to the two clusters of one owner, and on every device some owner receives exactly 64; each cluster holds at most 1024 invoices, and in every draw both clusters of some owner hold exactly 1024.
All inputs are finite; a program needn't handle non-finite values.
Results may differ from a plain program's by a relative error of at most 0.0035.
Values may be sent and summed in bfloat16 or wider, within the bound.
No kernel may reach another device: no remote copies, remote signals or barrier semaphores. Data moves between devices by JAX's collectives and lax.ppermute only.
A program may use at most 64 MiB of HBM per device.

v0:
```python
import jax
import jax.numpy as jnp
from jax import lax
from jax.sharding import PartitionSpec as P

TAU = 40.0


def unit_rows(rows):
    values = rows.astype(jnp.float32)
    return (values * lax.rsqrt(jnp.sum(values * values, axis=1, keepdims=True) + 1e-06)).astype(
        jnp.bfloat16
    )


def cluster_result(rows, units, present):
    capacity, width = rows.shape
    block = capacity // 4
    totals = [jnp.zeros((block, width), jnp.float32) for index in range(4)]
    masses = [jnp.zeros((block,), jnp.float32) for index in range(4)]
    inner = jnp.arange(block, dtype=jnp.int32)
    for left in range(4):
        for right in range(left, 4):
            units_left = units[left * block : (left + 1) * block]
            units_right = units[right * block : (right + 1) * block]
            rows_left = rows[left * block : (left + 1) * block]
            rows_right = rows[right * block : (right + 1) * block]
            keep = (
                present[left * block : (left + 1) * block][:, None]
                & present[right * block : (right + 1) * block][None, :]
            )
            if left == right:
                keep = keep & (inner[:, None] != inner[None, :])

            def scored(
                unused,
                units_left=units_left,
                units_right=units_right,
                rows_left=rows_left,
                rows_right=rows_right,
                keep=keep,
                diagonal=left == right,
            ):
                scores = jnp.dot(units_left, units_right.T, preferred_element_type=jnp.float32)
                weight = jnp.where(keep, jnp.exp(TAU * scores), jnp.zeros((), jnp.float32)).astype(
                    jnp.bfloat16
                )
                wide = weight.astype(jnp.float32)
                total_left = jnp.dot(weight, rows_right, preferred_element_type=jnp.float32)
                mass_left = jnp.sum(wide, axis=1)
                if diagonal:
                    return (
                        total_left,
                        mass_left,
                        jnp.zeros_like(total_left),
                        jnp.zeros_like(mass_left),
                    )
                total_right = lax.dot_general(
                    weight, rows_left, (((0,), (0,)), ((), ())), preferred_element_type=jnp.float32
                )
                return (total_left, mass_left, total_right, jnp.sum(wide, axis=0))

            parts = scored(None)
            totals[left] = totals[left] + parts[0]
            masses[left] = masses[left] + parts[1]
            if left != right:
                totals[right] = totals[right] + parts[2]
                masses[right] = masses[right] + parts[3]
    total = jnp.concatenate(totals, axis=0)
    mass = jnp.concatenate(masses, axis=0)
    return (rows.astype(jnp.float32) - total / (1.0 + mass)[:, None]).astype(jnp.bfloat16)


def on_device(embedding, cluster_of):
    rows_here, width = embedding.shape
    time_count = lax.axis_size("tm")
    owner_count = lax.axis_size("clus")
    owners = time_count * owner_count
    slot = 2 * rows_here // owners
    owner = cluster_of // 2
    hits = (owner[:, None] == jnp.arange(owners, dtype=jnp.int32)[None, :]).astype(jnp.int32)
    rank = jnp.sum(jnp.cumsum(hits, axis=0) * hits, axis=1) - 1
    target = owner * slot + rank
    outgoing = jnp.zeros((owners * slot, width), jnp.bfloat16).at[target].set(embedding)
    labels = jnp.full((owners * slot,), -1, jnp.int32).at[target].set(cluster_of)
    arrived, arrived_labels = (
        lax.all_to_all(
            outgoing.reshape(owners, slot, width),
            ("tm", "clus"),
            split_axis=0,
            concat_axis=0,
            tiled=True,
        ),
        lax.all_to_all(
            labels.reshape(owners, slot), ("tm", "clus"), split_axis=0, concat_axis=0, tiled=True
        ),
    )
    arrived = arrived.reshape(owners * slot, width)
    arrived_labels = arrived_labels.reshape(owners * slot)
    present = arrived_labels >= 0
    local = arrived_labels % 2
    member = (
        (local[:, None] == jnp.arange(2, dtype=jnp.int32)[None, :]) & present[:, None]
    ).astype(jnp.int32)
    place = jnp.sum(jnp.cumsum(member, axis=0) * member, axis=1) - 1
    position = jnp.where(present, local * rows_here + place, 2 * rows_here)
    grouped = jnp.zeros((2 * rows_here, width), jnp.bfloat16).at[position].set(arrived, mode="drop")
    filled = jnp.zeros((2 * rows_here,), jnp.bool_).at[position].set(True, mode="drop")
    units = unit_rows(grouped)
    results = []
    for cluster in range(2):
        rows_cluster = grouped[cluster * rows_here : (cluster + 1) * rows_here]
        units_cluster = units[cluster * rows_here : (cluster + 1) * rows_here]
        filled_cluster = filled[cluster * rows_here : (cluster + 1) * rows_here]
        results.append(cluster_result(rows_cluster, units_cluster, filled_cluster))
    merged = jnp.concatenate(results, axis=0)
    answers = jnp.take(merged, position, axis=0, mode="fill", fill_value=0)
    returned = lax.all_to_all(
        answers.reshape(owners, slot, width),
        ("tm", "clus"),
        split_axis=0,
        concat_axis=0,
        tiled=True,
    )
    returned = returned.reshape(owners * slot, width)
    return returned[target]


def solution(mesh):
    return jax.shard_map(
        on_device,
        mesh=mesh,
        in_specs=(P(("tm", "clus"), None), P(("tm", "clus"))),
        out_specs=P(("tm", "clus"), None),
        check_vma=False,
    )
```

profile of v0, /device:TPU:0, one launch (start us, length us, event | category | flops | bytes accessed | tf_op | source)
XLA Modules:
  0.0 155.6 jit_solution(4508203598809221913)
XLA Ops:
  0.0 0.7 add_select_fusion.3
  0.7 9.0 %reduce-window.14 = s32[32,8,128]{2,1,0:T(8,128)S(1)} reduce-window(s32[32,8,128]{2,1,0:T(8,128)S(1)} %fusion.80, s32[]{:T(128)} %constant.66.clone.1), window={size=1x1x128 pad=0_0x0_0x127_0}, to_apply=%region_0.1 | reduce-window | flops 4161536 | bytes 262148 | tf_op jit(solution)/shard_map/reduce-window
  10.2 0.7 broadcast_clamp_fusion.1
  10.9 4.5 %scatter_custom_fusion = s32[2048]{0:T(1024)S(1)} fusion(s32[1024]{0:T(1024)S(1)} %get-tuple-element.30, s32[1024]{0:T(1024)} %param.3, s32[]{:T(128)} %constant.64.clone.1), kind=kCustom, calls=%fused_computation.293 | custom fusion | bytes 8704 | tf_op jit(solution)/shard_map/scatter | solution.py:85
  15.4 0.7 all_to_all.12
  16.1 7.3 %all-to-all-start = ((s32[32,1,64]{2,1,0:T(1,128)}), s32[32,1,64]{2,1,0:T(1,128)S(1)}, u32[]{:S(2)}, u32[]{:S(2)}) async-start(s32[32,1,64]{2,1,0:T(1,128)} %all_to_all.12), calls=%async_computation | async-start | bytes 32768 | tf_op jit(solution)/shard_map/all_to_all | solution.py:94
  23.4 6.8 %scatter_custom_fusion.1 = bf16[2048,384]{1,0:T(8,128)(2,1)} fusion(s32[1024]{0:T(1024)S(1)} %get-tuple-element.30, bf16[1024,384]{1,0:T(8,128)(2,1)} %param.2, bf16[]{:T(256)} %constant.72.clone.1), kind=kCustom, calls=%fused_computation.124 | custom fusion | bytes 1573376 | tf_op jit(solution)/shard_map/scatter | solution.py:84
  30.2 0.3 all-to-all-done
  30.5 5.6 %all-to-all-start.1 = ((bf16[32,64,384]{2,1,0:T(8,128)(2,1)}), bf16[32,64,384]{2,1,0:T(8,128)(2,1)S(1)}, u32[]{:S(2)}, u32[]{:S(2)}) async-start(bf16[32,64,384]{2,1,0:T(8,128)(2,1)} %bitcast.7), calls=%async_computation.1 | async-start | bytes 3145728 | tf_op jit(solution)/shard_map/all_to_all | solution.py:87
  36.2 0.6 reduce-window.16
  37.2 0.5 broadcast.330
  37.7 0.7 reduce.9
  38.8 9.3 %scatter_custom_fusion.3 = pred[2048]{0:T(1024)(128)(4,1)S(1)} fusion(s32[2048]{0:T(1024)S(1)} %bitcast.79, pred[2048]{0:T(1024)(128)(4,1)S(1)} %broadcast.263, pred[]{:T(512)} %constant.73.clone.1), kind=kCustom, calls=%fused_computation.296 | custom fusion | bytes 2049 | tf_op jit(solution)/shard_map/scatter | solution.py:108
  48.1 26.8 %all-to-all-done.1 = bf16[32,64,384]{2,1,0:T(8,128)(2,1)S(1)} async-done(((bf16[32,64,384]{2,1,0:T(8,128)(2,1)}), bf16[32,64,384]{2,1,0:T(8,128)(2,1)S(1)}, u32[]{:S(2)}, u32[]{:S(2)}) %all-to-all-start.1) | async-done | bytes 1572896 | tf_op jit(solution)/shard_map/all_to_all | solution.py:87
  74.9 9.9 %scatter_custom_fusion.2 = bf16[2048,384]{1,0:T(8,128)(2,1)S(1)} fusion(s32[2048]{0:T(1024)S(1)} %bitcast.81, bf16[2048,384]{1,0:T(8,128)(2,1)S(1)} %bitcast.73, bf16[]{:T(256)} %constant.72.clone.1), kind=kCustom, calls=%fused_computation.122 | custom fusion | bytes 1572866 | tf_op jit(solution)/shard_map/scatter | solution.py:107
  84.8 0.4 fusion
  85.2 0.3 fusion.1
  85.6 0.3 convert_reduce_fusion.30
  85.9 0.3 convert_reduce_fusion.29
  86.1 0.4 convert_reduce_fusion.17
  86.5 0.3 convert_reduce_fusion.28
  86.8 0.4 convert_reduce_fusion.15
  87.1 0.3 convert_reduce_fusion.31
  87.4 0.4 convert_reduce_fusion.23
  87.8 0.4 convert_reduce_fusion.13
  88.1 0.4 convert_reduce_fusion.19
  88.5 0.4 convert_reduce_fusion.21
  88.8 0.3 convert_reduce_fusion.26
  89.1 0.3 convert_reduce_fusion.25
  89.4 0.4 convert_reduce_fusion.5
  89.8 0.3 convert_reduce_fusion.24
  90.1 0.4 convert_reduce_fusion.3
  90.4 0.3 convert_reduce_fusion.27
  90.7 0.4 convert_reduce_fusion.11
  91.1 0.4 convert_reduce_fusion.1
  91.4 0.4 convert_reduce_fusion.7
  91.8 0.4 convert_reduce_fusion.9
  93.3 0.3 convolution_add_fusion.10
  95.3 0.3 convolution_add_fusion.7
  95.6 0.3 convolution_add_fusion.6
  96.8 0.3 convolution_add_fusion.22
  97.3 0.3 convolution_add_fusion.21
  98.7 0.3 convolution_add_fusion.20
  100.2 1.4 fusion.3
  101.7 7.5 %gather_fusion = bf16[2048,384]{1,0:T(8,128)(2,1)S(1)} fusion(bf16[2048,384]{1,0:T(8,128)(2,1)S(1)} %pad_maximum_fusion, s32[2048]{0:T(1024)S(1)} %broadcast_clamp_fusion), kind=kCustom, calls=%fused_computation | custom fusion | bytes 3153920 | tf_op jit(solution)/shard_map/jit(_take)/gather | solution.py:117
  109.2 0.5 broadcast_select_fusion
  109.7 40.9 %all_to_all.19 = bf16[32,64,384]{2,1,0:T(8,128)(2,1)S(1)} all-to-all(bf16[32,64,384]{2,1,0:T(8,128)(2,1)S(1)} %broadcast_select_fusion), channel_id=1, replica_groups=mesh['tm'=4,'clus'=8] {'tm','clus'}, dimensions={0} | all-to-all | bytes 3145728 | tf_op jit(solution)/shard_map/all_to_all | solution.py:118
  150.6 5.0 %gather_fusion.1 = bf16[1024,384]{1,0:T(8,128)(2,1)} fusion(bf16[2048,384]{1,0:T(8,128)(2,1)S(1)} %bitcast.71, s32[1024]{0:T(1024)S(1)} %get-tuple-element.29), kind=kCustom, calls=%fused_computation.1 | custom fusion | bytes 1576960 | tf_op jit(solution)/shard_map/gather | solution.py:126
  (61 shorter events, 7.8 us)
Async XLA Ops:
  16.1 14.4 %all-to-all-start = ((s32[32,1,64]{2,1,0:T(1,128)}), s32[32,1,64]{2,1,0:T(1,128)S(1)}, u32[]{:S(2)}, u32[]{:S(2)}) async-start(s32[32,1,64]{2,1,0:T(1,128)} %all_to_all.12), calls=%async_computation | async-start | bytes 32768 | tf_op jit(solution)/shard_map/all_to_all | solution.py:94
  30.5 44.4 %all-to-all-start.1 = ((bf16[32,64,384]{2,1,0:T(8,128)(2,1)}), bf16[32,64,384]{2,1,0:T(8,128)(2,1)S(1)}, u32[]{:S(2)}, u32[]{:S(2)}) async-start(bf16[32,64,384]{2,1,0:T(8,128)(2,1)} %bitcast.7), calls=%async_computation.1 | async-start | bytes 3145728 | tf_op jit(solution)/shard_map/all_to_all | solution.py:87
where the time goes:
time: 156 us
  local copies, waits for them, and re-layouts  44.9 us (29%)
  blocking collectives  40.9 us (26%)
  waiting for transfers between devices  27.1 us (17%)
  other arithmetic  15.1 us (10%)
  matrix products  14.2 us (9%)
  starting transfers between devices  12.9 us (8%)
    all_to_all x1, blocking collectives, on_device(): lax.all_to_all(answers.reshape(owners, slot, width), ('tm', 'clus'), spli...  40.9 us
    all_to_all x1, waiting for transfers between devices, on_device(): lax.all_to_all(outgoing.reshape(owners, slot, width), ('tm', 'clus'), spl...  26.8 us
    another operation x5, other arithmetic  9.93 us
    scatter x1, local copies, waits for them, and re-layouts, on_device(): jnp.zeros((2 * rows_here, width), jnp.bfloat16).at[position]  9.9 us
    scatter x1, local copies, waits for them, and re-layouts, on_device(): jnp.zeros((2 * rows_here,), jnp.bool_).at[position].set(True, mode='drop')  9.29 us
    gather x1, local copies, waits for them, and re-layouts, on_device(): answers = jnp.take(merged, position, axis=0, mode='fill', fill_value=0)  7.46 us
    all_to_all x1, starting transfers between devices, on_device(): lax.all_to_all(labels.reshape(owners, slot), ('tm', 'clus'), split_axis=0...  7.3 us
    scatter x1, local copies, waits for them, and re-layouts, on_device(): jnp.zeros((owners * slot, width), jnp.bfloat16).at[target].set(embedding)  6.8 us
  transfers between devices with their start and end apart: 2, of which 2 were waited for; matrix products, arithmetic and copies ran while one was open for 12% of the time, Pallas kernels for 0%

commit v1 on v0

v1 whole, which is shorter than its diff:
```python
import functools
import math

import jax
import jax.numpy as jnp
from jax import lax
from jax.experimental import pallas as pl
from jax.experimental.pallas import tpu as pltpu
from jax.sharding import PartitionSpec as P

TAU = 40.0
LANES = 128
HEAD = 8
BLOCK = 512
VMEM_LIMIT = 32 * 1024 * 1024


def one_hot(mask):
    return jnp.where(mask, 1.0, 0.0).astype(jnp.bfloat16)


def copies_of(source_ref, target_ref, semaphores):
    pieces = semaphores.shape[0]
    each = source_ref.shape[0] // pieces
    spans = [pl.ds(i * each, each) for i in range(pieces)]
    return [
        pltpu.make_async_copy(source_ref.at[span], target_ref.at[span], semaphores.at[i])
        for i, span in enumerate(spans)
    ]


def route_kernel(
    owners, slot, half, cluster_hbm_ref, rows_hbm_ref, out_ref, column_ref,
    cluster_ref, rows_ref, cluster_arrival, rows_arrival,
):
    ids_copy = pltpu.make_async_copy(cluster_hbm_ref, cluster_ref, cluster_arrival)
    ids_copy.start()
    rows_copies = copies_of(rows_hbm_ref, rows_ref, rows_arrival)
    for copy in rows_copies:
        copy.start()
    groups = cluster_ref.shape[0]
    planes = rows_ref.shape[1] // LANES
    ids_copy.wait()
    cluster = cluster_ref[...]
    owner = cluster // 2
    low, side = owner % half, (owner // half) % 2
    cluster = 2 * (owner - low - side * half + 2 * low + side) + cluster % 2
    ids = lax.broadcasted_iota(jnp.int32, (2 * owners, LANES), 0)
    members = [ids == cluster[g : g + 1, :] for g in range(groups)]
    before = lax.broadcasted_iota(jnp.int32, (LANES, 2 * LANES), 0)
    lane = lax.broadcasted_iota(jnp.int32, (LANES, 2 * LANES), 1)
    counter = one_hot((before < lane) | (lane >= LANES))
    odd = ids % 2 == 1
    start = ((ids // 2) * slot + jnp.where(odd, slot - 1, 0)).astype(jnp.float32)
    total = jnp.zeros(ids.shape, jnp.float32)
    targets = []
    for g in range(groups):
        counted = jnp.dot(one_hot(members[g]), counter, preferred_element_type=jnp.float32)
        rank = counted[:, :LANES] + total
        place = start + jnp.where(odd, -rank, rank)
        targets.append(jnp.sum(jnp.where(members[g], place, 0.0), axis=0, keepdims=True))
        total = total + counted[:, LANES:]
    target = jnp.concatenate(targets, axis=0)
    column_ref[...] = target.T.astype(jnp.int32)
    target = target.astype(jnp.int32)
    upper = lax.broadcasted_iota(jnp.int32, (HEAD, LANES), 0) < HEAD // 2
    for o in range(owners):
        out_ref[o, planes * slot :, :] = jnp.where(
            upper, total[2 * o : 2 * o + 1, :], total[2 * o + 1 : 2 * o + 2, :]
        ).astype(jnp.bfloat16)
    for copy in rows_copies:
        copy.wait()
    for b in range(owners * slot // BLOCK):
        places = lax.broadcasted_iota(jnp.int32, (BLOCK, LANES), 0) + b * BLOCK
        pick = jnp.concatenate(
            [one_hot(places == target[g : g + 1, :]) for g in range(groups)], axis=1
        )
        sent = jnp.dot(pick, rows_ref[...], preferred_element_type=jnp.float32)
        sent = sent.astype(jnp.bfloat16)
        first, count = b * BLOCK // slot, BLOCK // slot
        for j in range(planes):
            out_ref[first : first + count, j * slot : (j + 1) * slot, :] = sent[
                :, j * LANES : (j + 1) * LANES
            ].reshape(count, slot, LANES)


def weights(left, right, diagonal):
    scores = lax.dot_general(
        left, right, (((1,), (1,)), ((), ())), preferred_element_type=jnp.float32
    )
    weight = jnp.exp2(scores * (TAU * math.log2(math.e)))
    if diagonal:
        here = lax.broadcasted_iota(jnp.int32, (BLOCK, BLOCK), 0)
        there = lax.broadcasted_iota(jnp.int32, (BLOCK, BLOCK), 1)
        weight = jnp.where(here == there, 0.0, weight)
    return weight.astype(jnp.bfloat16)


def summed(weight, value, transposed=False):
    return lax.dot_general(
        weight,
        value,
        (((0 if transposed else 1,), (0,)), ((), ())),
        preferred_element_type=jnp.float32,
    )


def owner_kernel(owners, slot, rows_ref, out_ref, unit_ref, value_ref, left_ref, right_ref):
    size, width = unit_ref.shape
    planes = width // LANES
    part = slot // 2
    side = size // 2
    lane = lax.broadcasted_iota(jnp.int32, (part, LANES), 1)
    rank = lax.broadcasted_iota(jnp.int32, (part, LANES), 0).astype(jnp.float32)
    most = jnp.zeros((HEAD, LANES), jnp.float32)

    def counts_of(s):
        counts = rows_ref[s, planes * slot :, :].astype(jnp.float32)
        return counts, counts[:1, :], counts[HEAD // 2 : HEAD // 2 + 1, :]

    for s in range(owners):
        counts, first, second = counts_of(s)
        most = jnp.maximum(most, counts)
        for h in range(2):
            here = pl.ds(h * side + s * part, part)
            there = (rank + h * part < first) | (rank + h * part >= slot - second)
            value_ref[here, width:] = one_hot(there & (lane == 0))
            for j in range(planes):
                at = j * slot + h * part
                value_ref[here, j * LANES : (j + 1) * LANES] = rows_ref[s, at : at + part, :]
    for b in range(size // BLOCK):
        span = slice(b * BLOCK, (b + 1) * BLOCK)
        wide = value_ref[span, :width].astype(jnp.float32)
        unit_ref[span, :] = (
            wide * lax.rsqrt(jnp.sum(wide * wide, axis=1, keepdims=True) + 1e-06)
        ).astype(jnp.bfloat16)

    def finish(b, total):
        mass = total[:, width : width + 1]
        span = slice(b * BLOCK, (b + 1) * BLOCK)
        result = value_ref[span, :width].astype(jnp.float32) - total[:, :width] / (1.0 + mass)
        result = result.astype(jnp.bfloat16)
        h, s = b * BLOCK // side, b * BLOCK % side // part
        for i in range(BLOCK // part):
            at = (s + i) * slot + h * part
            out_ref[at : at + part, :] = result[i * part : (i + 1) * part, :]

    blocks = side // BLOCK
    spans = [slice(b * BLOCK, (b + 1) * BLOCK) for b in range(2 * blocks)]
    for h in range(2):
        mine = range(h * blocks, (h + 1) * blocks)
        totals = {b: 0.0 for b in mine}
        for b in mine:
            for k in range(b, mine[-1] + 1):
                weight = weights(unit_ref[spans[b], :], unit_ref[spans[k], :], b == k)
                totals[b] = totals[b] + summed(weight, value_ref[spans[k], :])
                if k != b:
                    totals[k] = totals[k] + summed(weight, value_ref[spans[b], :], True)
            finish(b, totals[b])

    @pl.when(jnp.max(most) > part)
    def all_pairs():
        for s in range(owners):
            counts, first, second = counts_of(s)
            for h in range(2):
                here = pl.ds(h * side + s * part, part)
                sign = jnp.where(rank + h * part < first, 1.0, -1.0)
                left = jnp.where(lane == 0, sign, jnp.where(lane == 1, 1.0, 0.0))
                right = jnp.where(lane == 0, 2.0 * sign, jnp.where(lane == 1, -2.0, 0.0))
                left_ref[here, width:] = left.astype(jnp.bfloat16)
                right_ref[here, width:] = right.astype(jnp.bfloat16)
        left_ref[:, :width] = unit_ref[...]
        right_ref[:, :width] = unit_ref[...]
        for b in range(2 * blocks):
            total = 0.0
            for k in range(2 * blocks):
                weight = weights(left_ref[spans[b], :], right_ref[spans[k], :], b == k)
                total = total + summed(weight, value_ref[spans[k], :])
            finish(b, total)


def return_kernel(column_ref, rows_ref, out_ref, held_ref, leaving):
    column = column_ref[...]
    places = lax.broadcasted_iota(jnp.int32, (LANES, rows_ref.shape[0]), 1)
    each = BLOCK // LANES
    copies = copies_of(held_ref, out_ref, leaving)
    ready = len(copies) * BLOCK // held_ref.shape[0]
    for b in range(column.shape[1] // each):
        pick = jnp.concatenate(
            [one_hot(places == column[:, g : g + 1]) for g in range(b * each, (b + 1) * each)],
            axis=0,
        )
        held_ref[b * BLOCK : (b + 1) * BLOCK, :] = jnp.dot(
            pick, rows_ref[...], preferred_element_type=jnp.float32
        ).astype(jnp.bfloat16)
        for copy in copies[b * ready : (b + 1) * ready]:
            copy.start()
    for copy in copies:
        copy.wait()


VMEM = pl.BlockSpec(memory_space=pltpu.VMEM)
HBM = pl.BlockSpec(memory_space=pltpu.HBM)
PARAMS = pltpu.CompilerParams(vmem_limit_bytes=VMEM_LIMIT)


def on_device(embedding, cluster_of):
    rows_here, width = embedding.shape
    axes = ("tm", "clus")
    owners = lax.axis_size("tm") * lax.axis_size("clus")
    half = lax.axis_size("clus") // 2
    slot = 2 * rows_here // owners
    size = owners * slot
    groups = rows_here // LANES
    padded = width + LANES
    depth = slot * (width // LANES) + HEAD
    outgoing, column = pl.pallas_call(
        functools.partial(route_kernel, owners, slot, half),
        out_shape=(
            jax.ShapeDtypeStruct((owners, depth, LANES), jnp.bfloat16),
            jax.ShapeDtypeStruct((LANES, groups), jnp.int32),
        ),
        in_specs=[HBM, HBM],
        out_specs=(VMEM, VMEM),
        scratch_shapes=[
            pltpu.VMEM((groups, LANES), jnp.int32),
            pltpu.VMEM((rows_here, width), jnp.bfloat16),
            pltpu.SemaphoreType.DMA,
            pltpu.SemaphoreType.DMA((4,)),
        ],
        compiler_params=PARAMS,
        name="route",
    )(
        pltpu.with_memory_space_constraint(cluster_of.reshape(groups, LANES), pltpu.HBM),
        pltpu.with_memory_space_constraint(embedding, pltpu.HBM),
    )

    order = [
        start + side * half + low
        for start in range(0, owners, 2 * half)
        for low in range(half)
        for side in range(2)
    ]

    def exchange(rows):
        return lax.all_to_all(
            rows, axes, split_axis=0, concat_axis=0, tiled=True, axis_index_groups=[order]
        )

    arrived = exchange(outgoing)
    answers = pl.pallas_call(
        functools.partial(owner_kernel, owners, slot),
        out_shape=jax.ShapeDtypeStruct((size, width), jnp.bfloat16),
        in_specs=[VMEM],
        out_specs=VMEM,
        scratch_shapes=[pltpu.VMEM((size, width), jnp.bfloat16)]
        + [pltpu.VMEM((size, padded), jnp.bfloat16)] * 3,
        compiler_params=PARAMS,
        name="pairs",
    )(arrived)
    returned = exchange(answers.reshape(owners, slot, width)).reshape(size, width)
    return pl.pallas_call(
        return_kernel,
        out_shape=jax.ShapeDtypeStruct((rows_here, width), jnp.bfloat16),
        in_specs=[VMEM, VMEM],
        out_specs=pl.BlockSpec(memory_space=pl.ANY),
        scratch_shapes=[
            pltpu.VMEM((rows_here, width), jnp.bfloat16),
            pltpu.SemaphoreType.DMA((8,)),
        ],
        compiler_params=PARAMS,
        name="back",
    )(column, returned)


def solution(mesh):
    return jax.shard_map(
        on_device,
        mesh=mesh,
        in_specs=(P(("tm", "clus"), None), P(("tm", "clus"))),
        out_specs=P(("tm", "clus"), None),
        check_vma=False,
    )
```

time: 156 us -> 98.4 us (0.63)
  blocking collectives: 40.9 us -> 86.4 us
  local copies, waits for them, and re-layouts: 44.9 us -> 0 us
  waiting for transfers between devices: 27.1 us -> 0 us
  other arithmetic: 15.1 us -> 0 us
  matrix products: 14.2 us -> 0 us
  starting transfers between devices: 12.9 us -> 0 us
  Pallas kernels: 0 us -> 11.7 us
    all_to_all x1 -> x2, blocking collectives: 40.9 us -> 86.4 us  [exchange(): lax.all_to_all(rows, axes, split_axis=0, concat_axis=0, tiled=True, axis_...]
    scatter x4 -> x0, local copies, waits for them, and re-layouts: 30.5 us -> none  [the longest x1 9.9 us: on_device(): jnp.zeros((2 * rows_here, width), jnp.bfloat16).at[position]]
    all_to_all x2 -> x0, waiting for transfers between devices: 27.1 us -> none  [the longest x1 26.8 us: on_device(): lax.all_to_all(outgoing.reshape(owners, slot, width), ('tm', 'clus'), spl...]
    dot_general x52 -> x0, matrix products: 14.2 us -> none  [the longest x20 6.52 us: scored(): jnp.dot(units_left, units_right.T, preferred_element_type=jnp.float32)]
    all_to_all x2 -> x0, starting transfers between devices: 12.9 us -> none  [the longest x1 7.3 us: on_device(): lax.all_to_all(labels.reshape(owners, slot), ('tm', 'clus'), split_axis=0...]
    gather x2 -> x0, local copies, waits for them, and re-layouts: 12.5 us -> none  [the longest x1 7.46 us: on_device(): answers = jnp.take(merged, position, axis=0, mode='fill', fill_value=0)]
    pallas_call x0 -> x3, Pallas kernels: none -> 11.7 us  [the longest x1 4.75 us: on_device(): pl.pallas_call(functools.partial(owner_kernel, owners, slot), out_shape=j...]
    another operation x5 -> x0, other arithmetic: 9.93 us -> none
  transfers between devices with their start and end apart: 2 -> 0, of which waited for: 2 -> 0; matrix products, arithmetic and copies ran while one was open for 12% -> 0% of each run, Pallas kernels for 0% -> 0%
where the time goes in v1:
time: 98.4 us; the launch traced here: 98.2 us
  blocking collectives  86.4 us (88%)
  Pallas kernels  11.7 us (12%)
    all_to_all x2, blocking collectives, exchange(): lax.all_to_all(rows, axes, split_axis=0, concat_axis=0, tiled=True, axis_...  86.4 us
    pallas_call x1, Pallas kernels, on_device(): pl.pallas_call(functools.partial(owner_kernel, owners, slot), out_shape=j...  4.75 us
    pallas_call x1, Pallas kernels, on_device(): pl.pallas_call(functools.partial(route_kernel, owners, slot, half), out_s...  3.72 us
    pallas_call x1, Pallas kernels, on_device(): pl.pallas_call(return_kernel, out_shape=jax.ShapeDtypeStruct((rows_here,...  3.18 us

profile of v1, /device:TPU:0, one launch (start us, length us, event | category | flops | bytes accessed | tf_op | source)
XLA Modules:
  0.0 98.2 jit_solution(11252783149646611219)
XLA Ops:
  0.0 3.7 %route.1 = (bf16[32,200,128]{2,1,0:T(8,128)(2,1)S(1)}, s32[128,8]{1,0:T(8,128)S(1)}) custom-call(s32[8,128]{1,0:T(8,128)} %bitcast.5, bf16[1024,384]{1,0:T(8,128)(2,1)} %rows_hbm_ref.1), custom_call_target="tpu_custom_call" | custom-call | tf_op jit(solution)/shard_map/route/pallas_call | solution.py:217
  3.7 46.0 %all_to_all.10.rows_ref = bf16[32,200,128]{2,1,0:T(8,128)(2,1)S(1)} all-to-all(bf16[32,200,128]{2,1,0:T(8,128)(2,1)S(1)} %get-tuple-element.8), channel_id=1, replica_groups={{0,4,1,5,2,6,3,7,8,12,9,13,10,14,11,15,16,20,17,21,18,22,19,23,24,28,25..., dimensions={0} | all-to-all | bytes 3276800 | tf_op jit(solution)/shard_map/all_to_all | solution.py:246
  49.7 4.7 %pairs.1 = bf16[2048,384]{1,0:T(8,128)(2,1)S(1)} custom-call(bf16[32,200,128]{2,1,0:T(8,128)(2,1)S(1)} %all_to_all.10.rows_ref), custom_call_target="tpu_custom_call" | custom-call | tf_op jit(solution)/shard_map/pairs/pallas_call | solution.py:251
  54.5 40.4 %all_to_all.11 = bf16[32,64,384]{2,1,0:T(8,128)(2,1)S(1)} all-to-all(bf16[32,64,384]{2,1,0:T(8,128)(2,1)S(1)} %bitcast.4), channel_id=1, replica_groups={{0,4,1,5,2,6,3,7,8,12,9,13,10,14,11,15,16,20,17,21,18,22,19,23,24,28,25..., dimensions={0} | all-to-all | bytes 3145728 | tf_op jit(solution)/shard_map/all_to_all | solution.py:246
  94.9 3.2 %back.1 = bf16[1024,384]{1,0:T(8,128)(2,1)} custom-call(s32[128,8]{1,0:T(8,128)S(1)} %get-tuple-element.7.column_ref, bf16[2048,384]{1,0:T(8,128)(2,1)S(1)} %bitcast.3), custom_call_target="tpu_custom_call" | custom-call | tf_op jit(solution)/shard_map/back/pallas_call | solution.py:262

commit v2 on v1

--- a/solution.py
+++ b/solution.py
@@ -12,6 +12,7 @@
 LANES = 128
 HEAD = 8
 BLOCK = 512
+TILE = 256
 VMEM_LIMIT = 32 * 1024 * 1024
 
 
@@ -90,22 +91,15 @@
     )
     weight = jnp.exp2(scores * (TAU * math.log2(math.e)))
     if diagonal:
-        here = lax.broadcasted_iota(jnp.int32, (BLOCK, BLOCK), 0)
-        there = lax.broadcasted_iota(jnp.int32, (BLOCK, BLOCK), 1)
+        here = lax.broadcasted_iota(jnp.int32, weight.shape, 0)
+        there = lax.broadcasted_iota(jnp.int32, weight.shape, 1)
         weight = jnp.where(here == there, 0.0, weight)
     return weight.astype(jnp.bfloat16)
 
 
-def summed(weight, value, transposed=False):
-    return lax.dot_general(
-        weight,
-        value,
-        (((0 if transposed else 1,), (0,)), ((), ())),
-        preferred_element_type=jnp.float32,
-    )
-
-
-def owner_kernel(owners, slot, rows_ref, out_ref, unit_ref, value_ref, left_ref, right_ref):
+def owner_kernel(
+    owners, slot, rows_ref, out_ref, unit_ref, value_ref, left_ref, right_ref, *weight_refs
+):
     size, width = unit_ref.shape
     planes = width // LANES
     part = slot // 2
@@ -147,16 +141,23 @@
 
     blocks = side // BLOCK
     spans = [slice(b * BLOCK, (b + 1) * BLOCK) for b in range(2 * blocks)]
+    tiles = [slice(at, at + TILE) for at in range(0, side, TILE)]
     for h in range(2):
-        mine = range(h * blocks, (h + 1) * blocks)
-        totals = {b: 0.0 for b in mine}
-        for b in mine:
-            for k in range(b, mine[-1] + 1):
-                weight = weights(unit_ref[spans[b], :], unit_ref[spans[k], :], b == k)
-                totals[b] = totals[b] + summed(weight, value_ref[spans[k], :])
-                if k != b:
-                    totals[k] = totals[k] + summed(weight, value_ref[spans[b], :], True)
-            finish(b, totals[b])
+        weight_ref = weight_refs[h]
+        units = [unit_ref[h * side + t.start : h * side + t.stop, :] for t in tiles]
+        for k, across in enumerate(tiles):
+            for b, down in enumerate(tiles[: k + 1]):
+                weight = weights(units[b], units[k], b == k)
+                weight_ref[down, across] = weight
+                if b != k:
+                    weight_ref[across, down] = weight.T
+        for b in range(blocks):
+            total = jnp.dot(
+                weight_ref[spans[b], :],
+                value_ref[h * side : (h + 1) * side, :],
+                preferred_element_type=jnp.float32,
+            )
+            finish(h * blocks + b, total)
 
     @pl.when(jnp.max(most) > part)
     def all_pairs():
@@ -175,7 +176,9 @@
             total = 0.0
             for k in range(2 * blocks):
                 weight = weights(left_ref[spans[b], :], right_ref[spans[k], :], b == k)
-                total = total + summed(weight, value_ref[spans[k], :])
+                total = total + jnp.dot(
+                    weight, value_ref[spans[k], :], preferred_element_type=jnp.float32
+                )
             finish(b, total)
 
 
@@ -254,7 +257,8 @@
         in_specs=[VMEM],
         out_specs=VMEM,
         scratch_shapes=[pltpu.VMEM((size, width), jnp.bfloat16)]
-        + [pltpu.VMEM((size, padded), jnp.bfloat16)] * 3,
+        + [pltpu.VMEM((size, padded), jnp.bfloat16)] * 3
+        + [pltpu.VMEM((size // 2, size // 2), jnp.bfloat16)] * 2,
         compiler_params=PARAMS,
         name="pairs",
     )(arrived)

time: 98.4 us -> 98.1 us (level)
  no operation moved by 1% of the time
where the time goes in v2:
time: 98.1 us; the launch traced here: 97.9 us
  blocking collectives  86.4 us (88%)
  Pallas kernels  11.4 us (12%)
    all_to_all x2, blocking collectives, exchange(): lax.all_to_all(rows, axes, split_axis=0, concat_axis=0, tiled=True, axis_...  86.4 us
    pallas_call x1, Pallas kernels, on_device(): pl.pallas_call(functools.partial(owner_kernel, owners, slot), out_shape=j...  4.48 us
    pallas_call x1, Pallas kernels, on_device(): pl.pallas_call(functools.partial(route_kernel, owners, slot, half), out_s...  3.72 us
    pallas_call x1, Pallas kernels, on_device(): pl.pallas_call(return_kernel, out_shape=jax.ShapeDtypeStruct((rows_here,...  3.18 us

profile of v2, /device:TPU:0, one launch (start us, length us, event | category | flops | bytes accessed | tf_op | source)
XLA Modules:
  0.0 97.9 jit_solution(3938836892714389147)
XLA Ops:
  0.0 3.7 %route.1 = (bf16[32,200,128]{2,1,0:T(8,128)(2,1)S(1)}, s32[128,8]{1,0:T(8,128)S(1)}) custom-call(s32[8,128]{1,0:T(8,128)} %bitcast.5, bf16[1024,384]{1,0:T(8,128)(2,1)} %rows_hbm_ref.1), custom_call_target="tpu_custom_call" | custom-call | tf_op jit(solution)/shard_map/route/pallas_call | solution.py:220
  3.7 46.0 %all_to_all.10.rows_ref = bf16[32,200,128]{2,1,0:T(8,128)(2,1)S(1)} all-to-all(bf16[32,200,128]{2,1,0:T(8,128)(2,1)S(1)} %get-tuple-element.8), channel_id=1, replica_groups={{0,4,1,5,2,6,3,7,8,12,9,13,10,14,11,15,16,20,17,21,18,22,19,23,24,28,25..., dimensions={0} | all-to-all | bytes 3276800 | tf_op jit(solution)/shard_map/all_to_all | solution.py:249
  49.7 4.5 %pairs.1 = bf16[2048,384]{1,0:T(8,128)(2,1)S(1)} custom-call(bf16[32,200,128]{2,1,0:T(8,128)(2,1)S(1)} %all_to_all.10.rows_ref), custom_call_target="tpu_custom_call" | custom-call | tf_op jit(solution)/shard_map/pairs/pallas_call | solution.py:254
  54.2 40.4 %all_to_all.11 = bf16[32,64,384]{2,1,0:T(8,128)(2,1)S(1)} all-to-all(bf16[32,64,384]{2,1,0:T(8,128)(2,1)S(1)} %bitcast.4), channel_id=1, replica_groups={{0,4,1,5,2,6,3,7,8,12,9,13,10,14,11,15,16,20,17,21,18,22,19,23,24,28,25..., dimensions={0} | all-to-all | bytes 3145728 | tf_op jit(solution)/shard_map/all_to_all | solution.py:249
  94.6 3.2 %back.1 = bf16[1024,384]{1,0:T(8,128)(2,1)} custom-call(s32[128,8]{1,0:T(8,128)S(1)} %get-tuple-element.7.column_ref, bf16[2048,384]{1,0:T(8,128)(2,1)S(1)} %bitcast.3), custom_call_target="tpu_custom_call" | custom-call | tf_op jit(solution)/shard_map/back/pallas_call | solution.py:266

commit v3 on v2

--- a/solution.py
+++ b/solution.py
@@ -31,8 +31,8 @@
 
 
 def route_kernel(
-    owners, slot, half, cluster_hbm_ref, rows_hbm_ref, out_ref, column_ref,
-    cluster_ref, rows_ref, cluster_arrival, rows_arrival,
+    owners, slot, half, cluster_hbm_ref, rows_hbm_ref, out_ref, target_ref,
+    cluster_ref, rows_ref, turned_ref, cluster_arrival, rows_arrival,
 ):
     ids_copy = pltpu.make_async_copy(cluster_hbm_ref, cluster_ref, cluster_arrival)
     ids_copy.start()
@@ -62,8 +62,8 @@
         targets.append(jnp.sum(jnp.where(members[g], place, 0.0), axis=0, keepdims=True))
         total = total + counted[:, LANES:]
     target = jnp.concatenate(targets, axis=0)
-    column_ref[...] = target.T.astype(jnp.int32)
     target = target.astype(jnp.int32)
+    target_ref[...] = target
     upper = lax.broadcasted_iota(jnp.int32, (HEAD, LANES), 0) < HEAD // 2
     for o in range(owners):
         out_ref[o, planes * slot :, :] = jnp.where(
@@ -71,13 +71,17 @@
         ).astype(jnp.bfloat16)
     for copy in rows_copies:
         copy.wait()
+    for at in range(0, rows_ref.shape[0], BLOCK):
+        turned_ref[:, at : at + BLOCK] = rows_ref[at : at + BLOCK, :].T
     for b in range(owners * slot // BLOCK):
         places = lax.broadcasted_iota(jnp.int32, (BLOCK, LANES), 0) + b * BLOCK
         pick = jnp.concatenate(
             [one_hot(places == target[g : g + 1, :]) for g in range(groups)], axis=1
         )
-        sent = jnp.dot(pick, rows_ref[...], preferred_element_type=jnp.float32)
-        sent = sent.astype(jnp.bfloat16)
+        sent = lax.dot_general(
+            turned_ref[...], pick, (((1,), (1,)), ((), ())), preferred_element_type=jnp.float32
+        )
+        sent = sent.astype(jnp.bfloat16).T
         first, count = b * BLOCK // slot, BLOCK // slot
         for j in range(planes):
             out_ref[first : first + count, j * slot : (j + 1) * slot, :] = sent[
@@ -98,7 +102,7 @@
 
 
 def owner_kernel(
-    owners, slot, rows_ref, out_ref, unit_ref, value_ref, left_ref, right_ref, *weight_refs
+    owners, slot, rows_ref, out_ref, unit_ref, value_ref, left_ref, right_ref, *refs
 ):
     size, width = unit_ref.shape
     planes = width // LANES
@@ -129,11 +133,7 @@
             wide * lax.rsqrt(jnp.sum(wide * wide, axis=1, keepdims=True) + 1e-06)
         ).astype(jnp.bfloat16)
 
-    def finish(b, total):
-        mass = total[:, width : width + 1]
-        span = slice(b * BLOCK, (b + 1) * BLOCK)
-        result = value_ref[span, :width].astype(jnp.float32) - total[:, :width] / (1.0 + mass)
-        result = result.astype(jnp.bfloat16)
+    def write(b, result):
         h, s = b * BLOCK // side, b * BLOCK % side // part
         for i in range(BLOCK // part):
             at = (s + i) * slot + h * part
@@ -143,7 +143,7 @@
     spans = [slice(b * BLOCK, (b + 1) * BLOCK) for b in range(2 * blocks)]
     tiles = [slice(at, at + TILE) for at in range(0, side, TILE)]
     for h in range(2):
-        weight_ref = weight_refs[h]
+        weight_ref, turned_ref = refs[h], refs[2 + h]
         units = [unit_ref[h * side + t.start : h * side + t.stop, :] for t in tiles]
         for k, across in enumerate(tiles):
             for b, down in enumerate(tiles[: k + 1]):
@@ -152,12 +152,16 @@
                 if b != k:
                     weight_ref[across, down] = weight.T
         for b in range(blocks):
+            span = spans[h * blocks + b]
+            turned_ref[:width, spans[b]] = value_ref[span, :width].T
+            turned_ref[width:, spans[b]] = value_ref[span, width:].T[: 2 * HEAD, :]
+        for b in range(blocks):
             total = jnp.dot(
-                weight_ref[spans[b], :],
-                value_ref[h * side : (h + 1) * side, :],
-                preferred_element_type=jnp.float32,
+                turned_ref[...], weight_ref[:, spans[b]], preferred_element_type=jnp.float32
             )
-            finish(h * blocks + b, total)
+            result = turned_ref[:width, spans[b]].astype(jnp.float32)
+            result = result - total[:width, :] / (1.0 + total[width : width + 1, :])
+            write(h * blocks + b, result.astype(jnp.bfloat16).T)
 
     @pl.when(jnp.max(most) > part)
     def all_pairs():
@@ -179,23 +183,27 @@
                 total = total + jnp.dot(
                     weight, value_ref[spans[k], :], preferred_element_type=jnp.float32
                 )
-            finish(b, total)
-
-
-def return_kernel(column_ref, rows_ref, out_ref, held_ref, leaving):
-    column = column_ref[...]
-    places = lax.broadcasted_iota(jnp.int32, (LANES, rows_ref.shape[0]), 1)
-    each = BLOCK // LANES
+            mass = total[:, width : width + 1]
+            result = value_ref[spans[b], :width].astype(jnp.float32)
+            write(b, (result - total[:, :width] / (1.0 + mass)).astype(jnp.bfloat16))
+
+
+def return_kernel(target_ref, rows_ref, out_ref, turned_ref, held_ref, leaving):
+    target = target_ref[...]
+    size, width = rows_ref.shape
+    for at in range(0, size, BLOCK):
+        turned_ref[:, at : at + BLOCK] = rows_ref[at : at + BLOCK, :].T
+    places = lax.broadcasted_iota(jnp.int32, (size, LANES), 0)
+    each = TILE // LANES
     copies = copies_of(held_ref, out_ref, leaving)
-    ready = len(copies) * BLOCK // held_ref.shape[0]
-    for b in range(column.shape[1] // each):
+    ready = len(copies) * TILE // held_ref.shape[0]
+    for b in range(held_ref.shape[0] // TILE):
         pick = jnp.concatenate(
-            [one_hot(places == column[:, g : g + 1]) for g in range(b * each, (b + 1) * each)],
-            axis=0,
-        )
-        held_ref[b * BLOCK : (b + 1) * BLOCK, :] = jnp.dot(
-            pick, rows_ref[...], preferred_element_type=jnp.float32
-        ).astype(jnp.bfloat16)
+            [one_hot(places == target[g : g + 1, :]) for g in range(b * each, (b + 1) * each)],
+            axis=1,
+        )
+        result = jnp.dot(turned_ref[...], pick, preferred_element_type=jnp.float32)
+        held_ref[b * TILE : (b + 1) * TILE, :] = result.astype(jnp.bfloat16).T
         for copy in copies[b * ready : (b + 1) * ready]:
             copy.start()
     for copy in copies:
@@ -217,17 +225,18 @@
     groups = rows_here // LANES
     padded = width + LANES
     depth = slot * (width // LANES) + HEAD
-    outgoing, column = pl.pallas_call(
+    outgoing, target = pl.pallas_call(
         functools.partial(route_kernel, owners, slot, half),
         out_shape=(
             jax.ShapeDtypeStruct((owners, depth, LANES), jnp.bfloat16),
-            jax.ShapeDtypeStruct((LANES, groups), jnp.int32),
+            jax.ShapeDtypeStruct((groups, LANES), jnp.int32),
         ),
         in_specs=[HBM, HBM],
         out_specs=(VMEM, VMEM),
         scratch_shapes=[
             pltpu.VMEM((groups, LANES), jnp.int32),
             pltpu.VMEM((rows_here, width), jnp.bfloat16),
+            pltpu.VMEM((width, rows_here), jnp.bfloat16),
             pltpu.SemaphoreType.DMA,
             pltpu.SemaphoreType.DMA((4,)),
         ],
@@ -258,7 +267,8 @@
         out_specs=VMEM,
         scratch_shapes=[pltpu.VMEM((size, width), jnp.bfloat16)]
         + [pltpu.VMEM((size, padded), jnp.bfloat16)] * 3
-        + [pltpu.VMEM((size // 2, size // 2), jnp.bfloat16)] * 2,
+        + [pltpu.VMEM((size // 2, size // 2), jnp.bfloat16)] * 2
+        + [pltpu.VMEM((width + 2 * HEAD, size // 2), jnp.bfloat16)] * 2,
         compiler_params=PARAMS,
         name="pairs",
     )(arrived)
@@ -269,12 +279,13 @@
         in_specs=[VMEM, VMEM],
         out_specs=pl.BlockSpec(memory_space=pl.ANY),
         scratch_shapes=[
+            pltpu.VMEM((width, size), jnp.bfloat16),
             pltpu.VMEM((rows_here, width), jnp.bfloat16),
             pltpu.SemaphoreType.DMA((8,)),
         ],
         compiler_params=PARAMS,
         name="back",
-    )(column, returned)
+    )(target, returned)
 
 
 def solution(mesh):

time: 98.1 us -> 97.1 us (0.990)
  Pallas kernels: 11.4 us -> 10.3 us
where the time goes in v3:
time: 97.1 us; the launch traced here: 96.9 us
  blocking collectives  86.4 us (89%)
  Pallas kernels  10.3 us (11%)
    all_to_all x2, blocking collectives, exchange(): lax.all_to_all(rows, axes, split_axis=0, concat_axis=0, tiled=True, axis_...  86.4 us
    pallas_call x1, Pallas kernels, on_device(): pl.pallas_call(functools.partial(owner_kernel, owners, slot), out_shape=j...  4.45 us
    pallas_call x1, Pallas kernels, on_device(): pl.pallas_call(functools.partial(route_kernel, owners, slot, half), out_s...  3.19 us
    pallas_call x1, Pallas kernels, on_device(): pl.pallas_call(return_kernel, out_shape=jax.ShapeDtypeStruct((rows_here,...  2.7 us

profile of v3, /device:TPU:0, one launch (start us, length us, event | category | flops | bytes accessed | tf_op | source)
XLA Modules:
  0.0 96.9 jit_solution(3935472806957734425)
XLA Ops:
  0.0 3.2 %route.1 = (bf16[32,200,128]{2,1,0:T(8,128)(2,1)S(1)}, s32[8,128]{1,0:T(8,128)S(1)}) custom-call(s32[8,128]{1,0:T(8,128)} %bitcast.5, bf16[1024,384]{1,0:T(8,128)(2,1)} %rows_hbm_ref.1), custom_call_target="tpu_custom_call" | custom-call | tf_op jit(solution)/shard_map/route/pallas_call | solution.py:228
  3.2 46.0 %all_to_all.10.rows_ref = bf16[32,200,128]{2,1,0:T(8,128)(2,1)S(1)} all-to-all(bf16[32,200,128]{2,1,0:T(8,128)(2,1)S(1)} %get-tuple-element.8), channel_id=1, replica_groups={{0,4,1,5,2,6,3,7,8,12,9,13,10,14,11,15,16,20,17,21,18,22,19,23,24,28,25..., dimensions={0} | all-to-all | bytes 3276800 | tf_op jit(solution)/shard_map/all_to_all | solution.py:258
  49.2 4.5 %pairs.1 = bf16[2048,384]{1,0:T(8,128)(2,1)S(1)} custom-call(bf16[32,200,128]{2,1,0:T(8,128)(2,1)S(1)} %all_to_all.10.rows_ref), custom_call_target="tpu_custom_call" | custom-call | tf_op jit(solution)/shard_map/pairs/pallas_call | solution.py:263
  53.7 40.4 %all_to_all.11 = bf16[32,64,384]{2,1,0:T(8,128)(2,1)S(1)} all-to-all(bf16[32,64,384]{2,1,0:T(8,128)(2,1)S(1)} %bitcast.4), channel_id=1, replica_groups={{0,4,1,5,2,6,3,7,8,12,9,13,10,14,11,15,16,20,17,21,18,22,19,23,24,28,25..., dimensions={0} | all-to-all | bytes 3145728 | tf_op jit(solution)/shard_map/all_to_all | solution.py:258
  94.0 2.7 %back.1 = bf16[1024,384]{1,0:T(8,128)(2,1)} custom-call(s32[8,128]{1,0:T(8,128)S(1)} %get-tuple-element.7.target_ref, bf16[2048,384]{1,0:T(8,128)(2,1)S(1)} %bitcast.3), custom_call_target="tpu_custom_call" | custom-call | tf_op jit(solution)/shard_map/back/pallas_call | solution.py:276

commit v4 on v3

--- a/solution.py
+++ b/solution.py
@@ -102,36 +102,24 @@
 
 
 def owner_kernel(
-    owners, slot, rows_ref, out_ref, unit_ref, value_ref, left_ref, right_ref, *refs
+    owners, slot, rows_ref, out_ref, value_ref, left_ref, right_ref, *refs
 ):
-    size, width = unit_ref.shape
+    unit_refs, weight_refs, turned_refs = refs[:2], refs[2:4], refs[4:]
+    size, width = value_ref.shape[0], value_ref.shape[1] - LANES
     planes = width // LANES
     part = slot // 2
     side = size // 2
-    lane = lax.broadcasted_iota(jnp.int32, (part, LANES), 1)
-    rank = lax.broadcasted_iota(jnp.int32, (part, LANES), 0).astype(jnp.float32)
-    most = jnp.zeros((HEAD, LANES), jnp.float32)
-
-    def counts_of(s):
-        counts = rows_ref[s, planes * slot :, :].astype(jnp.float32)
-        return counts, counts[:1, :], counts[HEAD // 2 : HEAD // 2 + 1, :]
-
-    for s in range(owners):
-        counts, first, second = counts_of(s)
-        most = jnp.maximum(most, counts)
-        for h in range(2):
-            here = pl.ds(h * side + s * part, part)
-            there = (rank + h * part < first) | (rank + h * part >= slot - second)
-            value_ref[here, width:] = one_hot(there & (lane == 0))
-            for j in range(planes):
-                at = j * slot + h * part
-                value_ref[here, j * LANES : (j + 1) * LANES] = rows_ref[s, at : at + part, :]
-    for b in range(size // BLOCK):
-        span = slice(b * BLOCK, (b + 1) * BLOCK)
-        wide = value_ref[span, :width].astype(jnp.float32)
-        unit_ref[span, :] = (
-            wide * lax.rsqrt(jnp.sum(wide * wide, axis=1, keepdims=True) + 1e-06)
-        ).astype(jnp.bfloat16)
+    blocks = side // BLOCK
+    spans = [slice(b * BLOCK, (b + 1) * BLOCK) for b in range(2 * blocks)]
+    tiles = [slice(at, at + TILE) for at in range(0, side, TILE)]
+    counts = [rows_ref[s, planes * slot :, :].astype(jnp.float32) for s in range(owners)]
+    most = functools.reduce(jnp.maximum, counts)
+    firsts = [c[:1, :] for c in counts]
+    seconds = [c[HEAD // 2 : HEAD // 2 + 1, :] for c in counts]
+
+    def plane(h, j):
+        at = j * slot + h * part
+        return rows_ref[:, at : at + part, :].reshape(side, LANES)
 
     def write(b, result):
         h, s = b * BLOCK // side, b * BLOCK % side // part
@@ -139,43 +127,72 @@
             at = (s + i) * slot + h * part
             out_ref[at : at + part, :] = result[i * part : (i + 1) * part, :]
 
-    blocks = side // BLOCK
-    spans = [slice(b * BLOCK, (b + 1) * BLOCK) for b in range(2 * blocks)]
-    tiles = [slice(at, at + TILE) for at in range(0, side, TILE)]
-    for h in range(2):
-        weight_ref, turned_ref = refs[h], refs[2 + h]
-        units = [unit_ref[h * side + t.start : h * side + t.stop, :] for t in tiles]
+    each = LANES // part
+    lane = lax.broadcasted_iota(jnp.int32, (1, LANES), 1)
+    def prepare(h):
+        rank = (lane % part).astype(jnp.float32) + h * part
+        for g in range(owners // each):
+            first, second = firsts[g * each], seconds[g * each]
+            for i in range(1, each):
+                first = jnp.where(lane < i * part, first, firsts[g * each + i])
+                second = jnp.where(lane < i * part, second, seconds[g * each + i])
+            there = one_hot((rank < first) | (rank >= slot - second))
+            turned_refs[h][width:, g * LANES : (g + 1) * LANES] = jnp.broadcast_to(
+                there, (2 * HEAD, LANES)
+            )
+        wide = [plane(h, j).astype(jnp.float32) for j in range(planes)]
+        square = functools.reduce(lambda a, b: a + b, [w * w for w in wide])
+        scale = lax.rsqrt(jnp.sum(square, axis=1, keepdims=True) + 1e-06)
+        for j in range(planes):
+            columns = slice(j * LANES, (j + 1) * LANES)
+            unit_refs[h][:, columns] = (wide[j] * scale).astype(jnp.bfloat16)
+            turned_refs[h][columns, :] = plane(h, j).T
+
+    def weigh(h):
+        units = [unit_refs[h][t, :] for t in tiles]
         for k, across in enumerate(tiles):
             for b, down in enumerate(tiles[: k + 1]):
                 weight = weights(units[b], units[k], b == k)
-                weight_ref[down, across] = weight
+                weight_refs[h][down, across] = weight
                 if b != k:
-                    weight_ref[across, down] = weight.T
-        for b in range(blocks):
-            span = spans[h * blocks + b]
-            turned_ref[:width, spans[b]] = value_ref[span, :width].T
-            turned_ref[width:, spans[b]] = value_ref[span, width:].T[: 2 * HEAD, :]
+                    weight_refs[h][across, down] = weight.T
+
+    def mix(h):
+        turned_ref = turned_refs[h]
         for b in range(blocks):
             total = jnp.dot(
-                turned_ref[...], weight_ref[:, spans[b]], preferred_element_type=jnp.float32
+                turned_ref[...], weight_refs[h][:, spans[b]], preferred_element_type=jnp.float32
             )
             result = turned_ref[:width, spans[b]].astype(jnp.float32)
             result = result - total[:width, :] / (1.0 + total[width : width + 1, :])
             write(h * blocks + b, result.astype(jnp.bfloat16).T)
 
+    prepare(0)
+    weigh(0)
+    prepare(1)
+    weigh(1)
+    mix(0)
+    mix(1)
+
     @pl.when(jnp.max(most) > part)
     def all_pairs():
-        for s in range(owners):
-            counts, first, second = counts_of(s)
-            for h in range(2):
+        column = lax.broadcasted_iota(jnp.int32, (part, LANES), 1)
+        for h in range(2):
+            rank = lax.broadcasted_iota(jnp.int32, (part, LANES), 0).astype(jnp.float32) + h * part
+            for s in range(owners):
                 here = pl.ds(h * side + s * part, part)
-                sign = jnp.where(rank + h * part < first, 1.0, -1.0)
-                left = jnp.where(lane == 0, sign, jnp.where(lane == 1, 1.0, 0.0))
-                right = jnp.where(lane == 0, 2.0 * sign, jnp.where(lane == 1, -2.0, 0.0))
+                mine = rank < firsts[s]
+                there = mine | (rank >= slot - seconds[s])
+                sign = jnp.where(mine, 1.0, -1.0)
+                left = jnp.where(column == 0, sign, jnp.where(column == 1, 1.0, 0.0))
+                right = jnp.where(column == 0, 2.0 * sign, jnp.where(column == 1, -2.0, 0.0))
                 left_ref[here, width:] = left.astype(jnp.bfloat16)
                 right_ref[here, width:] = right.astype(jnp.bfloat16)
-        left_ref[:, :width] = unit_ref[...]
-        right_ref[:, :width] = unit_ref[...]
+                value_ref[here, width:] = one_hot(there & (column == 0))
+            for j in range(planes):
+                value_ref[h * side : (h + 1) * side, j * LANES : (j + 1) * LANES] = plane(h, j)
+            left_ref[h * side : (h + 1) * side, :width] = unit_refs[h][...]
+            right_ref[h * side : (h + 1) * side, :width] = unit_refs[h][...]
         for b in range(2 * blocks):
             total = 0.0
             for k in range(2 * blocks):
@@ -265,8 +282,8 @@
         out_shape=jax.ShapeDtypeStruct((size, width), jnp.bfloat16),
         in_specs=[VMEM],
         out_specs=VMEM,
-        scratch_shapes=[pltpu.VMEM((size, width), jnp.bfloat16)]
-        + [pltpu.VMEM((size, padded), jnp.bfloat16)] * 3
+        scratch_shapes=[pltpu.VMEM((size, padded), jnp.bfloat16)] * 3
+        + [pltpu.VMEM((size // 2, width), jnp.bfloat16)] * 2
         + [pltpu.VMEM((size // 2, size // 2), jnp.bfloat16)] * 2
         + [pltpu.VMEM((width + 2 * HEAD, size // 2), jnp.bfloat16)] * 2,
         compiler_params=PARAMS,

time: 97.1 us -> 97.1 us (level)
  no operation moved by 1% of the time
where the time goes in v4:
time: 97.1 us; the launch traced here: 96.9 us
  blocking collectives  86.4 us (89%)
  Pallas kernels  10.4 us (11%)
    all_to_all x2, blocking collectives, exchange(): lax.all_to_all(rows, axes, split_axis=0, concat_axis=0, tiled=True, axis_...  86.4 us
    pallas_call x1, Pallas kernels, on_device(): pl.pallas_call(functools.partial(owner_kernel, owners, slot), out_shape=j...  4.5 us
    pallas_call x1, Pallas kernels, on_device(): pl.pallas_call(functools.partial(route_kernel, owners, slot, half), out_s...  3.19 us
    pallas_call x1, Pallas kernels, on_device(): pl.pallas_call(return_kernel, out_shape=jax.ShapeDtypeStruct((rows_here,...  2.7 us

profile of v4, /device:TPU:0, one launch (start us, length us, event | category | flops | bytes accessed | tf_op | source)
XLA Modules:
  0.0 96.9 jit_solution(12706566547469916074)
XLA Ops:
  0.0 3.2 %route.1 = (bf16[32,200,128]{2,1,0:T(8,128)(2,1)S(1)}, s32[8,128]{1,0:T(8,128)S(1)}) custom-call(s32[8,128]{1,0:T(8,128)} %bitcast.5, bf16[1024,384]{1,0:T(8,128)(2,1)} %rows_hbm_ref.1), custom_call_target="tpu_custom_call" | custom-call | tf_op jit(solution)/shard_map/route/pallas_call | solution.py:245
  3.2 46.0 %all_to_all.10.rows_ref = bf16[32,200,128]{2,1,0:T(8,128)(2,1)S(1)} all-to-all(bf16[32,200,128]{2,1,0:T(8,128)(2,1)S(1)} %get-tuple-element.8), channel_id=1, replica_groups={{0,4,1,5,2,6,3,7,8,12,9,13,10,14,11,15,16,20,17,21,18,22,19,23,24,28,25..., dimensions={0} | all-to-all | bytes 3276800 | tf_op jit(solution)/shard_map/all_to_all | solution.py:275
  49.2 4.5 %pairs.1 = bf16[2048,384]{1,0:T(8,128)(2,1)S(1)} custom-call(bf16[32,200,128]{2,1,0:T(8,128)(2,1)S(1)} %all_to_all.10.rows_ref), custom_call_target="tpu_custom_call" | custom-call | tf_op jit(solution)/shard_map/pairs/pallas_call | solution.py:280
  53.7 40.4 %all_to_all.11 = bf16[32,64,384]{2,1,0:T(8,128)(2,1)S(1)} all-to-all(bf16[32,64,384]{2,1,0:T(8,128)(2,1)S(1)} %bitcast.4), channel_id=1, replica_groups={{0,4,1,5,2,6,3,7,8,12,9,13,10,14,11,15,16,20,17,21,18,22,19,23,24,28,25..., dimensions={0} | all-to-all | bytes 3145728 | tf_op jit(solution)/shard_map/all_to_all | solution.py:275
  94.1 2.7 %back.1 = bf16[1024,384]{1,0:T(8,128)(2,1)} custom-call(s32[8,128]{1,0:T(8,128)S(1)} %get-tuple-element.7.target_ref, bf16[2048,384]{1,0:T(8,128)(2,1)S(1)} %bitcast.3), custom_call_target="tpu_custom_call" | custom-call | tf_op jit(solution)/shard_map/back/pallas_call | solution.py:293

commit v5 on v4

--- a/solution.py
+++ b/solution.py
@@ -44,8 +44,9 @@
     ids_copy.wait()
     cluster = cluster_ref[...]
     owner = cluster // 2
-    low, side = owner % half, (owner // half) % 2
-    cluster = 2 * (owner - low - side * half + 2 * low + side) + cluster % 2
+    row, side, low = owner // (2 * half), (owner // half) % 2, owner % half
+    place = ((row % 2) * half + low) * (owners // (4 * half)) + row // 2
+    cluster = 2 * (2 * place + side) + cluster % 2
     ids = lax.broadcasted_iota(jnp.int32, (2 * owners, LANES), 0)
     members = [ids == cluster[g : g + 1, :] for g in range(groups)]
     before = lax.broadcasted_iota(jnp.int32, (LANES, 2 * LANES), 0)
@@ -102,10 +103,9 @@
 
 
 def owner_kernel(
-    owners, slot, rows_ref, out_ref, value_ref, left_ref, right_ref, *refs
+    owners, slot, rows_ref, out_ref, unit_ref, value_ref, left_ref, right_ref, *refs
 ):
-    unit_refs, weight_refs, turned_refs = refs[:2], refs[2:4], refs[4:]
-    size, width = value_ref.shape[0], value_ref.shape[1] - LANES
+    size, width = unit_ref.shape
     planes = width // LANES
     part = slot // 2
     side = size // 2
@@ -129,7 +129,7 @@
 
     each = LANES // part
     lane = lax.broadcasted_iota(jnp.int32, (1, LANES), 1)
-    def prepare(h):
+    for h in range(2):
         rank = (lane % part).astype(jnp.float32) + h * part
         for g in range(owners // each):
             first, second = firsts[g * each], seconds[g * each]
@@ -137,7 +137,7 @@
                 first = jnp.where(lane < i * part, first, firsts[g * each + i])
                 second = jnp.where(lane < i * part, second, seconds[g * each + i])
             there = one_hot((rank < first) | (rank >= slot - second))
-            turned_refs[h][width:, g * LANES : (g + 1) * LANES] = jnp.broadcast_to(
+            refs[2 + h][width:, g * LANES : (g + 1) * LANES] = jnp.broadcast_to(
                 there, (2 * HEAD, LANES)
             )
         wide = [plane(h, j).astype(jnp.float32) for j in range(planes)]
@@ -145,34 +145,25 @@
         scale = lax.rsqrt(jnp.sum(square, axis=1, keepdims=True) + 1e-06)
         for j in range(planes):
             columns = slice(j * LANES, (j + 1) * LANES)
-            unit_refs[h][:, columns] = (wide[j] * scale).astype(jnp.bfloat16)
-            turned_refs[h][columns, :] = plane(h, j).T
-
-    def weigh(h):
-        units = [unit_refs[h][t, :] for t in tiles]
+            unit_ref[h * side : (h + 1) * side, columns] = (wide[j] * scale).astype(jnp.bfloat16)
+            refs[2 + h][columns, :] = plane(h, j).T
+
+    for h in range(2):
+        weight_ref, turned_ref = refs[h], refs[2 + h]
+        units = [unit_ref[h * side + t.start : h * side + t.stop, :] for t in tiles]
         for k, across in enumerate(tiles):
             for b, down in enumerate(tiles[: k + 1]):
                 weight = weights(units[b], units[k], b == k)
-                weight_refs[h][down, across] = weight
+                weight_ref[down, across] = weight
                 if b != k:
-                    weight_refs[h][across, down] = weight.T
-
-    def mix(h):
-        turned_ref = turned_refs[h]
+                    weight_ref[across, down] = weight.T
         for b in range(blocks):
             total = jnp.dot(
-                turned_ref[...], weight_refs[h][:, spans[b]], preferred_element_type=jnp.float32
+                turned_ref[...], weight_ref[:, spans[b]], preferred_element_type=jnp.float32
             )
             result = turned_ref[:width, spans[b]].astype(jnp.float32)
             result = result - total[:width, :] / (1.0 + total[width : width + 1, :])
             write(h * blocks + b, result.astype(jnp.bfloat16).T)
-
-    prepare(0)
-    weigh(0)
-    prepare(1)
-    weigh(1)
-    mix(0)
-    mix(1)
 
     @pl.when(jnp.max(most) > part)
     def all_pairs():
@@ -191,8 +182,8 @@
                 value_ref[here, width:] = one_hot(there & (column == 0))
             for j in range(planes):
                 value_ref[h * side : (h + 1) * side, j * LANES : (j + 1) * LANES] = plane(h, j)
-            left_ref[h * side : (h + 1) * side, :width] = unit_refs[h][...]
-            right_ref[h * side : (h + 1) * side, :width] = unit_refs[h][...]
+        left_ref[:, :width] = unit_ref[...]
+        right_ref[:, :width] = unit_ref[...]
         for b in range(2 * blocks):
             total = 0.0
             for k in range(2 * blocks):
@@ -265,9 +256,10 @@
     )
 
     order = [
-        start + side * half + low
-        for start in range(0, owners, 2 * half)
+        (2 * upper + lower) * 2 * half + side * half + low
+        for lower in range(2)
         for low in range(half)
+        for upper in range(owners // (4 * half))
         for side in range(2)
     ]
 
@@ -282,8 +274,8 @@
         out_shape=jax.ShapeDtypeStruct((size, width), jnp.bfloat16),
         in_specs=[VMEM],
         out_specs=VMEM,
-        scratch_shapes=[pltpu.VMEM((size, padded), jnp.bfloat16)] * 3
-        + [pltpu.VMEM((size // 2, width), jnp.bfloat16)] * 2
+        scratch_shapes=[pltpu.VMEM((size, width), jnp.bfloat16)]
+        + [pltpu.VMEM((size, padded), jnp.bfloat16)] * 3
         + [pltpu.VMEM((size // 2, size // 2), jnp.bfloat16)] * 2
         + [pltpu.VMEM((width + 2 * HEAD, size // 2), jnp.bfloat16)] * 2,
         compiler_params=PARAMS,

time: 97.1 us -> 99 us (1.020)
  blocking collectives: 86.4 us -> 88.5 us
    all_to_all x2, blocking collectives: 86.4 us -> 88.5 us  [exchange(): lax.all_to_all(rows, axes, split_axis=0, concat_axis=0, tiled=True, axis_...]
where the time goes in v5:
time: 99 us; the launch traced here: 98.9 us
  blocking collectives  88.5 us (89%)
  Pallas kernels  10.2 us (10%)
    all_to_all x2, blocking collectives, exchange(): lax.all_to_all(rows, axes, split_axis=0, concat_axis=0, tiled=True, axis_...  88.5 us
    pallas_call x1, Pallas kernels, on_device(): pl.pallas_call(functools.partial(owner_kernel, owners, slot), out_shape=j...  4.29 us
    pallas_call x1, Pallas kernels, on_device(): pl.pallas_call(functools.partial(route_kernel, owners, slot, half), out_s...  3.19 us
    pallas_call x1, Pallas kernels, on_device(): pl.pallas_call(return_kernel, out_shape=jax.ShapeDtypeStruct((rows_here,...  2.7 us

profile of v5, /device:TPU:0, one launch (start us, length us, event | category | flops | bytes accessed | tf_op | source)
XLA Modules:
  0.0 98.9 jit_solution(7686584933767067957)
XLA Ops:
  0.0 3.2 %route.1 = (bf16[32,200,128]{2,1,0:T(8,128)(2,1)S(1)}, s32[8,128]{1,0:T(8,128)S(1)}) custom-call(s32[8,128]{1,0:T(8,128)} %bitcast.5, bf16[1024,384]{1,0:T(8,128)(2,1)} %rows_hbm_ref.1), custom_call_target="tpu_custom_call" | custom-call | tf_op jit(solution)/shard_map/route/pallas_call | solution.py:236
  3.2 47.5 %all_to_all.10.rows_ref = bf16[32,200,128]{2,1,0:T(8,128)(2,1)S(1)} all-to-all(bf16[32,200,128]{2,1,0:T(8,128)(2,1)S(1)} %get-tuple-element.8), channel_id=1, replica_groups={{0,4,16,20,1,5,17,21,2,6,18,22,3,7,19,23,8,12,24,28,9,13,25,29,10,14,26..., dimensions={0} | all-to-all | bytes 3276800 | tf_op jit(solution)/shard_map/all_to_all | solution.py:267
  50.7 4.3 %pairs.1 = bf16[2048,384]{1,0:T(8,128)(2,1)S(1)} custom-call(bf16[32,200,128]{2,1,0:T(8,128)(2,1)S(1)} %all_to_all.10.rows_ref), custom_call_target="tpu_custom_call" | custom-call | tf_op jit(solution)/shard_map/pairs/pallas_call | solution.py:272
  55.0 41.0 %all_to_all.11 = bf16[32,64,384]{2,1,0:T(8,128)(2,1)S(1)} all-to-all(bf16[32,64,384]{2,1,0:T(8,128)(2,1)S(1)} %bitcast.4), channel_id=1, replica_groups={{0,4,16,20,1,5,17,21,2,6,18,22,3,7,19,23,8,12,24,28,9,13,25,29,10,14,26..., dimensions={0} | all-to-all | bytes 3145728 | tf_op jit(solution)/shard_map/all_to_all | solution.py:267
  96.0 2.7 %back.1 = bf16[1024,384]{1,0:T(8,128)(2,1)} custom-call(s32[8,128]{1,0:T(8,128)S(1)} %get-tuple-element.7.target_ref, bf16[2048,384]{1,0:T(8,128)(2,1)S(1)} %bitcast.3), custom_call_target="tpu_custom_call" | custom-call | tf_op jit(solution)/shard_map/back/pallas_call | solution.py:285
